TPU v7x, 32 devices: a whole 2x2x4 slice. The times are simulated.
32 devices in a mesh: groups: 2 (over y), patch: 4 (over z), sub: 2 (over x), lane: 2 (over core).
Axes of the slice: x: 2, y: 2, z: 4, core: 2. Of those that a mesh axis runs over, the one named last changes fastest.
Arguments:
- node_latents: float32 [4096, 512], P(('groups', 'patch', 'sub')), parts along dimension 0, may hold values from -6 to 6
- edge_latents: bfloat16 [32768, 512], P(('groups', 'patch', 'sub', 'lane')), parts along dimension 0, may hold values from -6 to 6
- sender_slot: int32 [32768], P(('groups', 'patch', 'sub', 'lane')), parts along dimension 0, may hold values from 0 to 543, as said below
- receiver_slot: int32 [32768], P(('groups', 'patch', 'sub', 'lane')), parts along dimension 0, may hold values from 0 to 543
- near_send: int32 [32, 2, 128], P(('groups', 'patch', 'sub', 'lane')), parts along dimension 0, may hold values from 0 to 255, as said below
- far_send: int32 [32, 8, 4], P(('groups', 'patch', 'sub', 'lane')), parts along dimension 0, may hold values from 0 to 255, as said below
- w_edge_in: bfloat16 [1536, 512], replicated, may hold values from -0.15625 to 0.15625
- w_edge_out: bfloat16 [512, 512], replicated, may hold values from -0.25 to 0.25
- w_node_in: bfloat16 [1024, 512], replicated, may hold values from -0.1875 to 0.1875
- w_node_out: bfloat16 [512, 512], replicated, may hold values from -0.25 to 0.25
- edge_bias_in: float32 [512], replicated, may hold values from -3 to 3
- edge_bias_out: float32 [512], replicated, may hold values from -3 to 3
- edge_gain: float32 [512], replicated, may hold values from 0.5 to 1.5
- edge_shift: float32 [512], replicated, may hold values from -2 to 2
- node_bias_in: float32 [512], replicated, may hold values from -3 to 3
- node_bias_out: float32 [512], replicated, may hold values from -3 to 3
- node_gain: float32 [512], replicated, may hold values from 0.5 to 1.5
- node_shift: float32 [512], replicated, may hold values from -2 to 2
Outputs:
- node_new: float32 [4096, 512], P(('groups', 'patch', 'sub')), parts along dimension 0
- edge_new: bfloat16 [32768, 512], P(('groups', 'patch', 'sub', 'lane')), parts along dimension 0
There are 2 independent parts, one for each index of `groups`. A program takes and returns all parts, laid end to end along the dimension named above; an argument that names none is the same for every part. Nothing has to cross between parts.
Inputs may be any that keep to these rules, and one draw needn't show every extreme that they name: On every device, each of its 544 slots is named by at least one sender_slot or receiver_slot entry of that device. `near_send`: the 128 entries of one list are distinct local rows. `far_send`: the 4 entries of one list are distinct local rows.
All inputs are finite; a program needn't handle non-finite values.
Results may differ from a plain program's by a relative error of at most 0.005.
Values may be sent and summed in bfloat16 or wider, within the bound.
A program may use at most 64 MiB of HBM per device.

v0:
```python
import jax
import jax.numpy as jnp
from jax import lax
from jax.sharding import PartitionSpec as P


def passed_along(block, axis, distance):
    devices = range(lax.axis_size(axis))
    route = [((i - distance) % len(devices), i) for i in devices]
    return lax.ppermute(block, axis, route)


def norm_rows(values, gain_vec, shift_vec):
    average = jnp.mean(values, axis=-1, keepdims=True)
    centred = values - average
    variance = jnp.mean(centred * centred, axis=-1, keepdims=True)
    return centred * lax.rsqrt(variance + 1e-05) * gain_vec + shift_vec


def node_update(latent, summed, w_first, w_second, bias_first, bias_second, gain_vec, shift_vec):
    feat_width = latent.shape[1]
    latent_bf = latent.astype(jnp.bfloat16)
    preact = jnp.dot(latent_bf, w_first[:feat_width], preferred_element_type=jnp.float32)
    preact = (
        preact
        + jnp.dot(
            summed.astype(jnp.bfloat16), w_first[feat_width:], preferred_element_type=jnp.float32
        )
        + bias_first
    )
    hidden = jax.nn.silu(preact).astype(jnp.bfloat16)
    output = jnp.dot(hidden, w_second, preferred_element_type=jnp.float32) + bias_second
    return latent + norm_rows(output, gain_vec, shift_vec)


def per_device(
    node_latents,
    edge_latents,
    sender_slot,
    receiver_slot,
    near_send,
    far_send,
    w_edge_in,
    w_edge_out,
    w_node_in,
    w_node_out,
    edge_bias_in,
    edge_bias_out,
    edge_gain,
    edge_shift,
    node_bias_in,
    node_bias_out,
    node_gain,
    node_shift,
):
    feat_width = node_latents.shape[1]
    node_count = node_latents.shape[0]
    patch_count = lax.axis_size("patch")
    sub_count = lax.axis_size("sub")
    peer_count = patch_count * sub_count
    far_width = far_send.shape[2]
    node_bf = node_latents.astype(jnp.bfloat16)
    w_send = w_edge_in[feat_width : 2 * feat_width]
    w_recv = w_edge_in[2 * feat_width :]
    lent_ahead = node_bf[near_send[0, 0]]
    lent_behind = node_bf[near_send[0, 1]]
    near_count = lent_ahead.shape[0]
    from_prev = passed_along(lent_ahead, "patch", 1)
    from_next = passed_along(lent_behind, "patch", -1)
    far_lent = node_bf[far_send[0]]
    far_in = lax.all_to_all(
        far_lent, ("patch", "sub"), split_axis=0, concat_axis=0, tiled=True
    ).reshape(peer_count * far_width, node_bf.shape[1])
    ghost = jnp.concatenate([node_bf, from_prev, from_next, far_in], axis=0)
    ghost_send = jnp.dot(ghost, w_send, preferred_element_type=jnp.float32).astype(jnp.bfloat16)
    ghost_recv = jnp.dot(ghost, w_recv, preferred_element_type=jnp.float32).astype(jnp.bfloat16)
    preact = jnp.dot(edge_latents, w_edge_in[:feat_width], preferred_element_type=jnp.float32)
    preact = (
        preact
        + ghost_send[sender_slot].astype(jnp.float32)
        + ghost_recv[receiver_slot].astype(jnp.float32)
        + edge_bias_in
    )
    hidden = jax.nn.silu(preact).astype(jnp.bfloat16)
    message = norm_rows(
        jnp.dot(hidden, w_edge_out, preferred_element_type=jnp.float32) + edge_bias_out,
        edge_gain,
        edge_shift,
    )
    edge_new = (edge_latents.astype(jnp.float32) + message).astype(jnp.bfloat16)
    slot_sums = jax.ops.segment_sum(message, receiver_slot, num_segments=ghost.shape[0])
    own_sums = slot_sums[:node_count]
    prev_sums = slot_sums[node_count : node_count + near_count]
    next_sums = slot_sums[node_count + near_count : node_count + 2 * near_count]
    far_sums = slot_sums[node_count + 2 * near_count :].reshape(peer_count, far_width, feat_width)
    back_ahead = passed_along(prev_sums.astype(jnp.bfloat16), "patch", -1).astype(prev_sums.dtype)
    back_behind = passed_along(next_sums.astype(jnp.bfloat16), "patch", 1).astype(next_sums.dtype)
    far_back = lax.all_to_all(
        far_sums, ("patch", "sub"), split_axis=0, concat_axis=0, tiled=True
    ).reshape(peer_count * far_width, feat_width)
    target_rows = jnp.concatenate([near_send[0, 0], near_send[0, 1], far_send[0].reshape(-1)])
    returned = jnp.concatenate([back_ahead, back_behind, far_back], axis=0)
    summed = own_sums + jax.ops.segment_sum(returned, target_rows, num_segments=node_count)
    summed_all = lax.psum(summed, "lane")
    node_new = node_update(
        node_latents,
        summed_all,
        w_node_in,
        w_node_out,
        node_bias_in,
        node_bias_out,
        node_gain,
        node_shift,
    )
    return (node_new, edge_new)


def solution(mesh):
    in_specs = (
        P(("groups", "patch", "sub"), None),
        P(("groups", "patch", "sub", "lane"), None),
        P(("groups", "patch", "sub", "lane")),
        P(("groups", "patch", "sub", "lane")),
        P(("groups", "patch", "sub", "lane"), None, None),
        P(("groups", "patch", "sub", "lane"), None, None),
        P(),
        P(),
        P(),
        P(),
        P(),
        P(),
        P(),
        P(),
        P(),
        P(),
        P(),
        P(),
    )
    out_specs = (P(("groups", "patch", "sub"), None), P(("groups", "patch", "sub", "lane"), None))
    return jax.shard_map(
        per_device, mesh=mesh, in_specs=in_specs, out_specs=out_specs, check_vma=False
    )
```

profile of v0, /device:TPU:1, one launch (start us, length us, event | category | flops | bytes accessed | tf_op | source)
XLA Modules:
  0.0 77.6 jit_solution(3297357935486964657)
XLA Ops:
  0.7 1.2 %convert_element_type.39 = bf16[256,512]{1,0:T(8,128)(2,1)S(1)} convert(f32[256,512]{1,0:T(8,128)} %param.18) | non-fusion elementwise | flops 131072 | bytes 786432 | tf_op jit(solution)/shard_map/convert_element_type | solution.py:22
  2.7 0.8 %gather_fusion = bf16[128,512]{1,0:T(8,128)(2,1)S(1)} fusion(bf16[256,512]{1,0:T(8,128)(2,1)S(1)} %convert_element_type.39, s32[1024]{0:T(1024)S(1)} %pad_clamp_fusion.2), kind=kCustom, calls=%fused_computation | custom fusion | bytes 262656 | tf_op jit(solution)/shard_map/gather | solution.py:65
  3.5 2.2 %collective-permute-start = (bf16[128,512]{1,0:T(8,128)(2,1)S(1)}, bf16[128,512]{1,0:T(8,128)(2,1)S(1)}, u32[]{:S(2)}, u32[]{:S(2)}) collective-permute-start(bf16[128,512]{1,0:T(8,128)(2,1)S(1)} %gather_fusion), channel_id=1, source_target_pairs={{12,0},{0,4},{4,8},{8,12},{13,1},{1,5},{5,9},{9,13},{14,2},{2,6},{... | collective-permute-start | bytes 393224 | tf_op jit(solution)/shard_map/ppermute | solution.py:10
  6.6 2.1 %collective-permute-start.1 = (bf16[128,512]{1,0:T(8,128)(2,1)S(1)}, bf16[128,512]{1,0:T(8,128)(2,1)S(1)}, u32[]{:S(2)}, u32[]{:S(2)}) collective-permute-start(bf16[128,512]{1,0:T(8,128)(2,1)S(1)} %gather_fusion.1), channel_id=1, source_target_pairs={{4,0},{8,4},{12,8},{0,12},{5,1},{9,5},{13,9},{1,13},{6,2},{10,6},{... | collective-permute-start | bytes 393224 | tf_op jit(solution)/shard_map/ppermute | solution.py:10
  10.1 3.6 %all-to-all-start = ((bf16[8,4,512]{2,1,0:T(4,128)(2,1)}), bf16[8,4,512]{2,1,0:T(4,128)(2,1)S(1)}, u32[]{:S(2)}, u32[]{:S(2)}) async-start(bf16[8,4,512]{2,1,0:T(4,128)(2,1)} %reshape.149), calls=%async_computation | async-start | bytes 65536 | tf_op jit(solution)/shard_map/all_to_all | solution.py:71
  13.8 1.1 %fusion.18 = f32[256,512]{1,0:T(8,128)} fusion(bf16[256,512]{1,0:T(8,128)(2,1)S(1)} %convert_element_type.39, bf16[1024,512]{1,0:T(8,128)(2,1)S(1)} %copy-done.6), kind=kOutput, calls=%fused_computation.36 | convolution fusion | flops 134217728 | bytes 1310720 | tf_op jit(solution)/shard_map/dot_general | solution.py:23
  14.9 1.3 %copy.27 = bf16[1024,512]{0,1:T(8,128)(2,1)} copy(bf16[1024,512]{1,0:T(8,128)(2,1)S(1)} %copy-done.4) | data formatting | bytes 2097152 | tf_op args[1]
  16.2 3.1 %all-to-all-done = bf16[8,4,512]{2,1,0:T(4,128)(2,1)S(1)} async-done(((bf16[8,4,512]{2,1,0:T(4,128)(2,1)}), bf16[8,4,512]{2,1,0:T(4,128)(2,1)S(1)}, u32[]{:S(2)}, u32[]{:S(2)}) %all-to-all-start) | async-done | bytes 32800 | tf_op jit(solution)/shard_map/all_to_all | solution.py:71
  19.3 1.5 %convolution_convert_fusion.1 = bf16[544,512]{1,0:T(8,128)(2,1)S(1)} fusion(bf16[1536,512]{1,0:T(8,128)(2,1)} %param.24, bf16[32,512]{1,0:T(8,128)(2,1)S(1)} %reshape.129, bf16[128,512]{1,0:T(8,128)(2,1)S(1)} %collective-permute-done.1, bf16[128,512]{1,0:T(8,128)(2,1)S(1)} %collective-permute-done, bf16[256,512]{1,0:T(8,128)(2,1)S(1)} %convert_element_type.39), kind=kOutput, calls=%fused_computation.14 | convolution fusion | flops 287719424 | bytes 1638400 | tf_op jit(solution)/shard_map/dot_general | solution.py:75
  20.8 5.1 %gather_fusion.3 = bf16[1024,512]{1,0:T(8,128)(2,1)} fusion(bf16[544,512]{1,0:T(8,128)(2,1)S(1)} %convolution_convert_fusion.1, s32[1024]{0:T(1024)S(1)} %fusion.24), kind=kCustom, calls=%fused_computation.3 | custom fusion | bytes 2101248 | tf_op jit(solution)/shard_map/gather | solution.py:80
  25.9 1.5 %convolution_convert_fusion = bf16[544,512]{1,0:T(8,128)(2,1)S(1)} fusion(bf16[1536,512]{1,0:T(8,128)(2,1)} %param.24, bf16[32,512]{1,0:T(8,128)(2,1)S(1)} %reshape.129, bf16[128,512]{1,0:T(8,128)(2,1)S(1)} %collective-permute-done.1, bf16[128,512]{1,0:T(8,128)(2,1)S(1)} %collective-permute-done, bf16[256,512]{1,0:T(8,128)(2,1)S(1)} %convert_element_type.39), kind=kOutput, calls=%fused_computation.13 | convolution fusion | flops 287719424 | bytes 1638400 | tf_op jit(solution)/shard_map/dot_general | solution.py:76
  27.4 5.1 %gather_fusion.4 = bf16[1024,512]{1,0:T(8,128)(2,1)} fusion(bf16[544,512]{1,0:T(8,128)(2,1)S(1)} %convolution_convert_fusion, s32[1024]{0:T(1024)S(1)} %fusion.25), kind=kCustom, calls=%fused_computation.4 | custom fusion | bytes 2101248 | tf_op jit(solution)/shard_map/gather | solution.py:81
  32.5 3.6 %add_reduce_fusion = (f32[1024]{0:T(1024)S(1)}, f32[1024,512]{0,1:T(8,128)S(1)}) fusion(f32[512]{0:T(512)S(1)} %copy-done.7, bf16[512,512]{1,0:T(8,128)(2,1)S(1)} %copy-done, bf16[1024,512]{1,0:T(8,128)(2,1)} %gather_fusion.4, bf16[1024,512]{1,0:T(8,128)(2,1)} %gather_fusion.3, bf16[1024,512]{1,0:T(8,128)(2,1)} %param.19, f32[512]{0:T(512)S(1)} %copy-done.16, ...), kind=kOutput, calls=%fused_computation.11 | convolution fusion | flops 1080032256 | bytes 6299648 | tf_op jit(solution)/shard_map/dot_general | solution.py:86
  37.4 2.3 %add_convert_fusion = (bf16[1024,512]{0,1:T(8,128)(2,1)}, f32[1024,512]{0,1:T(8,128)}) fusion(bf16[1024,512]{0,1:T(8,128)(2,1)S(1)} %copy-done.2, f32[512]{0:T(512)S(1)} %copy-done.12, f32[512]{0:T(512)S(1)} %copy-done.13, f32[1024]{0:T(1024)S(1)} %add_rsqrt_fusion, f32[1024]{0:T(1024)S(1)} %broadcast_multiply_fusion, f32[1024,512]{0,1:T(8,128)S(1)} %get-tuple-element.15, ...), kind=kLoop, calls=%fused_computation.7 | loop fusion | flops 4194304 | bytes 6305792 | tf_op jit(solution)/shard_map/convert_element_type | solution.py:90
  39.7 2.9 %copy.25 = f32[1024,512]{1,0:T(8,128)} copy(f32[1024,512]{0,1:T(8,128)} %get-tuple-element.7) | data formatting | bytes 4194304 | tf_op jit(solution)/shard_map/add | solution.py:17
  42.6 7.5 %scatter_custom_fusion = f32[544,512]{1,0:T(8,128)S(1)} fusion(s32[1024]{0:T(1024)S(1)} %copy-done.10, f32[1024,512]{1,0:T(8,128)} %copy.25, f32[]{:T(128)} %constant.7.clone.1), kind=kCustom, calls=%fused_computation.27 | custom fusion | flops 524288 | bytes 1114624 | tf_op jit(solution)/shard_map/scatter-add | solution.py:91
  51.4 1.1 %collective-permute-start.3 = (bf16[128,512]{1,0:T(8,128)(2,1)}, bf16[128,512]{1,0:T(8,128)(2,1)S(1)}, u32[]{:S(2)}, u32[]{:S(2)}) collective-permute-start(bf16[128,512]{1,0:T(8,128)(2,1)} %get-tuple-element.9), channel_id=1, source_target_pairs={{12,0},{0,4},{4,8},{8,12},{13,1},{1,5},{5,9},{9,13},{14,2},{2,6},{... | collective-permute-start | bytes 393224 | tf_op jit(solution)/shard_map/ppermute | solution.py:10
  53.1 4.1 %all-to-all-start.1 = ((f32[8,4,512]{2,1,0:T(4,128)}), f32[8,4,512]{2,1,0:T(4,128)S(1)}, u32[]{:S(2)}, u32[]{:S(2)}) async-start(f32[8,4,512]{2,1,0:T(4,128)} %reshape.130), calls=%async_computation.1 | async-start | bytes 131072 | tf_op jit(solution)/shard_map/all_to_all | solution.py:98
  57.5 1.3 %copy.28 = bf16[1024,512]{1,0:T(8,128)(2,1)} copy(bf16[1024,512]{0,1:T(8,128)(2,1)S(1)} %copy-done.1) | data formatting | bytes 2097152
  58.9 4.1 %all-to-all-done.1 = f32[8,4,512]{2,1,0:T(4,128)S(1)} async-done(((f32[8,4,512]{2,1,0:T(4,128)}), f32[8,4,512]{2,1,0:T(4,128)S(1)}, u32[]{:S(2)}, u32[]{:S(2)}) %all-to-all-start.1) | async-done | bytes 65568 | tf_op jit(solution)/shard_map/all_to_all | solution.py:98
  63.1 2.6 %scatter_custom_fusion.1 = f32[256,512]{1,0:T(8,128)S(1)} fusion(f32[256,512]{1,0:T(8,128)S(1)} %slice.58, s32[288]{0:T(512)S(1)} %pad_add_fusion, f32[32,512]{1,0:T(8,128)S(1)} %reshape.131, f32[]{:T(128)} %constant.30, f32[128,512]{1,0:T(8,128)S(1)} %convert_element_type.46, f32[128,512]{1,0:T(8,128)S(1)} %convert_element_type.45), kind=kCustom, calls=%fused_computation.20 | custom fusion | flops 442368 | bytes 1114116 | tf_op jit(solution)/shard_map/scatter-add | solution.py:103
  65.7 8.7 %all-reduce.1 = bf16[256,512]{1,0:T(8,128)(2,1)S(1)} all-reduce(f32[256,512]{1,0:T(8,128)S(1)} %scatter_custom_fusion.1), channel_id=1, replica_groups=mesh['groups'=2,'patch'=4,'sub'=2,'lane'=2] {'lane'}, use_global_device_ids=true, to_apply=%region_4.5 | all-reduce | flops 131072 | bytes 786432 | tf_op jit(solution)/shard_map/psum | solution.py:104
  74.4 1.9 %fusion.35 = (f32[256]{0:T(256)S(1)}, f32[256,512]{1,0:T(8,128)S(1)}) fusion(f32[512]{0:T(512)S(1)} %copy-done.17, bf16[512,512]{1,0:T(8,128)(2,1)} %param.27, f32[256,512]{1,0:T(8,128)S(1)} %copy-done.5, bf16[1024,512]{1,0:T(8,128)(2,1)} %param.26, f32[512]{0:T(512)S(1)} %copy-done.18, bf16[256,512]{1,0:T(8,128)(2,1)S(1)} %all-reduce.1), kind=kOutput, calls=%fused_computation.65 | convolution fusion | flops 269614848 | bytes 2364416 | tf_op jit(solution)/shard_map/dot_general | solution.py:32
  76.6 1.0 %add_add_fusion = f32[256,512]{1,0:T(8,128)} fusion(f32[256,512]{1,0:T(8,128)S(1)} %copy-done.3, f32[256,512]{1,0:T(8,128)S(1)} %get-tuple-element.17, f32[512]{0:T(512)S(1)} %copy-done.14, f32[512]{0:T(512)S(1)} %copy-done.15, f32[256]{0:T(256)S(1)} %add_rsqrt_fusion.1, f32[256]{0:T(256)S(1)} %broadcast_multiply_fusion.1), kind=kLoop, calls=%fused_computation.29 | loop fusion | flops 655360 | bytes 1579008 | tf_op jit(solution)/shard_map/add | solution.py:33
  (74 shorter events, 6.7 us)
Async XLA Ops:
  0.6 31.9 %copy-start = (bf16[512,512]{1,0:T(8,128)(2,1)S(1)}, bf16[512,512]{1,0:T(8,128)(2,1)}, u32[]{:S(2)}) copy-start(bf16[512,512]{1,0:T(8,128)(2,1)} %param.25) | copy-start | bytes 1572868
  0.6 8.0 %copy-start.8 = (s32[1,8,4]{1,2,0:T(4,128)S(1)}, s32[1,8,4]{1,2,0:T(4,128)}, u32[]{:S(2)}) copy-start(s32[1,8,4]{1,2,0:T(4,128)} %param.23) | copy-start | bytes 388
  0.7 13.1 %copy-start.9 = (s32[1024]{0:T(1024)S(1)}, s32[1024]{0:T(1024)}, u32[]{:S(2)}) copy-start(s32[1024]{0:T(1024)} %param.20) | copy-start | bytes 12292
  0.7 13.1 %copy-start.6 = (bf16[1024,512]{1,0:T(8,128)(2,1)S(1)}, bf16[1024,512]{1,0:T(8,128)(2,1)}, u32[]{:S(2)}) copy-start(bf16[1024,512]{1,0:T(8,128)(2,1)} %param.26) | copy-start | bytes 3145732
  1.9 13.0 %copy-start.10 = (s32[1024]{0:T(1024)S(1)}, s32[1024]{0:T(1024)}, u32[]{:S(2)}) copy-start(s32[1024]{0:T(1024)} %param.21) | copy-start | bytes 12292
  1.9 13.0 %copy-start.4 = (bf16[1024,512]{1,0:T(8,128)(2,1)S(1)}, bf16[1024,512]{1,0:T(8,128)(2,1)}, u32[]{:S(2)}) copy-start(bf16[1024,512]{1,0:T(8,128)(2,1)} %param.19) | copy-start | bytes 3145732
  3.5 15.8 %collective-permute-start = (bf16[128,512]{1,0:T(8,128)(2,1)S(1)}, bf16[128,512]{1,0:T(8,128)(2,1)S(1)}, u32[]{:S(2)}, u32[]{:S(2)}) collective-permute-start(bf16[128,512]{1,0:T(8,128)(2,1)S(1)} %gather_fusion), channel_id=1, source_target_pairs={{12,0},{0,4},{4,8},{8,12},{13,1},{1,5},{5,9},{9,13},{14,2},{2,6},{... | collective-permute-start | bytes 393224 | tf_op jit(solution)/shard_map/ppermute | solution.py:10
  6.6 12.8 %collective-permute-start.1 = (bf16[128,512]{1,0:T(8,128)(2,1)S(1)}, bf16[128,512]{1,0:T(8,128)(2,1)S(1)}, u32[]{:S(2)}, u32[]{:S(2)}) collective-permute-start(bf16[128,512]{1,0:T(8,128)(2,1)S(1)} %gather_fusion.1), channel_id=1, source_target_pairs={{4,0},{8,4},{12,8},{0,12},{5,1},{9,5},{13,9},{1,13},{6,2},{10,6},{... | collective-permute-start | bytes 393224 | tf_op jit(solution)/shard_map/ppermute | solution.py:10
  10.1 9.2 %all-to-all-start = ((bf16[8,4,512]{2,1,0:T(4,128)(2,1)}), bf16[8,4,512]{2,1,0:T(4,128)(2,1)S(1)}, u32[]{:S(2)}, u32[]{:S(2)}) async-start(bf16[8,4,512]{2,1,0:T(4,128)(2,1)} %reshape.149), calls=%async_computation | async-start | bytes 65536 | tf_op jit(solution)/shard_map/all_to_all | solution.py:71
  27.4 5.1 %copy-start.7 = (f32[512]{0:T(512)S(1)}, f32[512]{0:T(512)}, u32[]{:S(2)}) copy-start(f32[512]{0:T(512)} %param.29) | copy-start | bytes 6148
  27.4 5.1 %copy-start.16 = (f32[512]{0:T(512)S(1)}, f32[512]{0:T(512)}, u32[]{:S(2)}) copy-start(f32[512]{0:T(512)} %param.28) | copy-start | bytes 6148
  36.2 1.2 %copy-start.2 = (bf16[1024,512]{0,1:T(8,128)(2,1)S(1)}, bf16[1024,512]{0,1:T(8,128)(2,1)}, u32[]{:S(2)}) copy-start(bf16[1024,512]{0,1:T(8,128)(2,1)} %copy.27) | copy-start | bytes 3145732
  36.2 1.2 %copy-start.12 = (f32[512]{0:T(512)S(1)}, f32[512]{0:T(512)}, u32[]{:S(2)}) copy-start(f32[512]{0:T(512)} %param.31) | copy-start | bytes 6148
  42.6 14.6 %copy-start.11 = (s32[1,2,128]{2,1,0:T(2,128)S(1)}, s32[1,2,128]{2,1,0:T(2,128)}, u32[]{:S(2)}) copy-start(s32[1,2,128]{2,1,0:T(2,128)} %param.22) | copy-start | bytes 3076
  50.2 7.3 %copy-start.1 = (bf16[1024,512]{0,1:T(8,128)(2,1)S(1)}, bf16[1024,512]{0,1:T(8,128)(2,1)}, u32[]{:S(2)}) copy-start(bf16[1024,512]{0,1:T(8,128)(2,1)} %get-tuple-element.6) | copy-start | bytes 3145732
  51.0 12.0 %collective-permute-start.2 = (bf16[128,512]{1,0:T(8,128)(2,1)}, bf16[128,512]{1,0:T(8,128)(2,1)S(1)}, u32[]{:S(2)}, u32[]{:S(2)}) collective-permute-start(bf16[128,512]{1,0:T(8,128)(2,1)} %get-tuple-element.8), channel_id=1, source_target_pairs={{4,0},{8,4},{12,8},{0,12},{5,1},{9,5},{13,9},{1,13},{6,2},{10,6},{... | collective-permute-start | bytes 393224 | tf_op jit(solution)/shard_map/ppermute | solution.py:10
  51.4 11.7 %collective-permute-start.3 = (bf16[128,512]{1,0:T(8,128)(2,1)}, bf16[128,512]{1,0:T(8,128)(2,1)S(1)}, u32[]{:S(2)}, u32[]{:S(2)}) collective-permute-start(bf16[128,512]{1,0:T(8,128)(2,1)} %get-tuple-element.9), channel_id=1, source_target_pairs={{12,0},{0,4},{4,8},{8,12},{13,1},{1,5},{5,9},{9,13},{14,2},{2,6},{... | collective-permute-start | bytes 393224 | tf_op jit(solution)/shard_map/ppermute | solution.py:10
  53.1 9.9 %all-to-all-start.1 = ((f32[8,4,512]{2,1,0:T(4,128)}), f32[8,4,512]{2,1,0:T(4,128)S(1)}, u32[]{:S(2)}, u32[]{:S(2)}) async-start(f32[8,4,512]{2,1,0:T(4,128)} %reshape.130), calls=%async_computation.1 | async-start | bytes 131072 | tf_op jit(solution)/shard_map/all_to_all | solution.py:98
  57.5 16.9 %copy-start.5 = (f32[256,512]{1,0:T(8,128)S(1)}, f32[256,512]{1,0:T(8,128)}, u32[]{:S(2)}) copy-start(f32[256,512]{1,0:T(8,128)} %fusion.18) | copy-start | bytes 1572868
  57.5 16.9 %copy-start.17 = (f32[512]{0:T(512)S(1)}, f32[512]{0:T(512)}, u32[]{:S(2)}) copy-start(f32[512]{0:T(512)} %param.33) | copy-start | bytes 6148
  57.5 16.9 %copy-start.18 = (f32[512]{0:T(512)S(1)}, f32[512]{0:T(512)}, u32[]{:S(2)}) copy-start(f32[512]{0:T(512)} %param.32) | copy-start | bytes 6148
  74.4 2.2 %copy-start.3 = (f32[256,512]{1,0:T(8,128)S(1)}, f32[256,512]{1,0:T(8,128)}, u32[]{:S(2)}) copy-start(f32[256,512]{1,0:T(8,128)} %param.18) | copy-start | bytes 1572868
  74.4 2.2 %copy-start.14 = (f32[512]{0:T(512)S(1)}, f32[512]{0:T(512)}, u32[]{:S(2)}) copy-start(f32[512]{0:T(512)} %param.35) | copy-start | bytes 6148
  74.4 2.2 %copy-start.15 = (f32[512]{0:T(512)S(1)}, f32[512]{0:T(512)}, u32[]{:S(2)}) copy-start(f32[512]{0:T(512)} %param.34) | copy-start | bytes 6148
  (1 other events, 1.2 us)
where the time goes:
time: 78.2 us; the launch traced here: 77.6 us
  local copies, waits for them, and re-layouts  21.4 us (27%)
  other arithmetic  16.1 us (21%)
  starting transfers between devices  13.5 us (17%)
  matrix products  9.65 us (12%)
  blocking collectives  8.68 us (11%)
  waiting for transfers between devices  7.24 us (9%)
  between operations  1.05 us (1%)
    psum x1, blocking collectives, per_device(): summed_all = lax.psum(summed, 'lane')  8.68 us
    scatter-add x1, other arithmetic, per_device(): jax.ops.segment_sum(message, receiver_slot, num_segments=ghost.shape[0])  7.52 us
    ppermute x4, starting transfers between devices, passed_along(): return lax.ppermute(block, axis, route)  5.75 us
    gather x1, local copies, waits for them, and re-layouts, per_device(): ghost_send[sender_slot].astype(jnp.float32)  5.08 us
    gather x1, local copies, waits for them, and re-layouts, per_device(): ghost_recv[receiver_slot].astype(jnp.float32)  5.08 us
    all_to_all x1, waiting for transfers between devices, per_device(): lax.all_to_all(far_sums, ('patch', 'sub'), split_axis=0, concat_axis=0, t...  4.15 us
    all_to_all x1, starting transfers between devices, per_device(): lax.all_to_all(far_sums, ('patch', 'sub'), split_axis=0, concat_axis=0, t...  4.14 us
    dot_general x1, matrix products, per_device(): jnp.dot(hidden, w_edge_out, preferred_element_type=jnp.float32)  3.65 us
  transfers between devices with their start and end apart: 6, of which 2 were waited for; matrix products, arithmetic and copies ran while one was open for 9% of the time, Pallas kernels for 0%

commit v1 on v0

v1 whole, which is shorter than its diff:
```python
import functools

import jax
import jax.numpy as jnp
from jax import lax
from jax.experimental import pallas as pl
from jax.experimental.pallas import tpu as pltpu
from jax.sharding import PartitionSpec as P

MESH = pl.DeviceIdType.MESH
F32 = jnp.float32
BF16 = jnp.bfloat16
LANES = 128
ROW_BLOCK = 256


def mm(a, b):
    return jnp.dot(a, b, preferred_element_type=F32)


def silu(v):
    half = 0.5 * v
    return half + half * jnp.tanh(half)


def norm_rows(values, gain_vec, shift_vec):
    average = jnp.mean(values, axis=-1, keepdims=True)
    centred = values - average
    variance = jnp.mean(centred * centred, axis=-1, keepdims=True)
    return centred * lax.rsqrt(variance + 1e-05) * gain_vec + shift_vec


def ones_where(mask):
    return jnp.where(mask, 1.0, 0.0).astype(BF16)


def iota(shape, dim):
    return lax.broadcasted_iota(jnp.int32, shape, dim)


def layer_kernel(
    dims,
    node_hbm, edge_hbm, wei_hbm, weo_hbm, wni_hbm, wno_hbm,
    snd_ref, rcv_ref, lend_ref,
    ebi, ebo, egain, eshift, nbi, nbo, ngain, nshift,
    node_out, edge_out,
    node_v, edge_v, wei, weo, wni, wno, node_bf,
    lend_sel, near_src, far_src, near_in, far_in,
    pick_own, pick_ghost, proj_own, proj_ghost, drop, pre, msg,
    near_bsrc, far_bsrc, near_back, far_back, lane_src, lane_in, own_sum,
    load_sem, store_sem, near_ssem, near_rsem, far_ssem, far_rsem,
    nback_ssem, nback_rsem, fback_ssem, fback_rsem, lane_ssem, lane_rsem,
):
    n_patch, n_sub, n_lane, near, far = dims
    peers = n_patch * n_sub
    far_rows = peers * far
    pack = far * (node_v.shape[1] // LANES)
    n_node, d = node_v.shape
    n_edge = edge_v.shape[0]
    col_parts = d // LANES

    loads = [
        pltpu.make_async_copy(src, dst, load_sem.at[i])
        for i, (src, dst) in enumerate(
            [(node_hbm, node_v), (wei_hbm, wei), (edge_hbm, edge_v),
             (weo_hbm, weo), (wni_hbm, wni), (wno_hbm, wno)]
        )
    ]
    for load in loads:
        load.start()

    p = lax.axis_index("patch")
    s = lax.axis_index("sub")
    ln = lax.axis_index("lane")
    g = p * n_sub + s
    nxt = lax.rem(p + 1, n_patch)
    prv = lax.rem(p + n_patch - 1, n_patch)
    other = n_lane - 1 - ln

    def each_peer(fn):
        if peers <= 16:
            for o in range(1, peers):
                fn(o)
        else:
            def body(o, c):
                fn(o)
                return c
            lax.fori_loop(1, peers, body, 0)

    def peer_id(q):
        return {"patch": lax.div(q, n_sub), "sub": lax.rem(q, n_sub)}

    barrier = pltpu.get_barrier_semaphore()

    def greet(o):
        pl.semaphore_signal(
            barrier, inc=1, device_id=peer_id(lax.rem(g + o, peers)), device_id_type=MESH
        )

    each_peer(greet)
    pl.semaphore_signal(barrier, inc=1, device_id={"lane": other}, device_id_type=MESH)

    def column_of(ref, start, width):
        row = ref[:, start:start + width]
        return jnp.transpose(jnp.broadcast_to(row, (LANES, width)))

    lent = 2 * near + far_rows
    for r0 in range(0, lent, LANES):
        col = column_of(lend_ref, r0, LANES)
        for c0 in range(0, n_node, LANES):
            lend_sel[r0:r0 + LANES, c0:c0 + LANES] = ones_where(
                col == iota((LANES, LANES), 1) + c0
            )

    def packer(j):
        r = iota((peers * pack, far_rows), 0)
        c = iota((peers * pack, far_rows), 1)
        return ones_where(r == c // far * pack + j * far + c % far)

    def unpacker(j):
        r = iota((far_rows, peers * pack), 0)
        c = iota((far_rows, peers * pack), 1)
        return ones_where(c == r // far * pack + j * far + r % far)

    def packed(rows):
        total = mm(packer(0), rows[:, :LANES])
        for j in range(1, col_parts):
            total = total + mm(packer(j), rows[:, j * LANES:(j + 1) * LANES])
        return total.astype(BF16)

    def unpacked(block):
        return jnp.concatenate(
            [mm(unpacker(j), block).astype(BF16) for j in range(col_parts)], axis=1
        )

    loads[0].wait()
    node_bf[...] = node_v[...].astype(BF16)
    near_src[...] = mm(lend_sel[:2 * near, :], node_bf[...]).astype(BF16)
    far_src[...] = packed(
        mm(lend_sel[2 * near:lent, :], node_bf[...]).astype(BF16)
    )

    pl.semaphore_wait(barrier, peers)

    def near_copy(i, src, dst, ssem, rsem, patch):
        return pltpu.make_async_remote_copy(
            src_ref=src.at[pl.ds(i * near, near)],
            dst_ref=dst.at[pl.ds(i * near, near)],
            send_sem=ssem.at[i],
            recv_sem=rsem.at[i],
            device_id={"patch": patch},
            device_id_type=MESH,
        )

    def far_copy(o, src, dst, ssem, rsem):
        q = lax.rem(g + o, peers)
        return pltpu.make_async_remote_copy(
            src_ref=src.at[pl.ds(pl.multiple_of(q * pack, pack), pack)],
            dst_ref=dst.at[pl.ds(pl.multiple_of(g * pack, pack), pack)],
            send_sem=ssem.at[o],
            recv_sem=rsem.at[o],
            device_id=peer_id(q),
            device_id_type=MESH,
        )

    def far_arrival(o, src, dst, ssem, rsem):
        q = lax.rem(g + peers - o, peers)
        return pltpu.make_async_remote_copy(
            src_ref=src.at[pl.ds(pl.multiple_of(q * pack, pack), pack)],
            dst_ref=dst.at[pl.ds(pl.multiple_of(q * pack, pack), pack)],
            send_sem=ssem.at[o],
            recv_sem=rsem.at[o],
            device_id=peer_id(q),
            device_id_type=MESH,
        )

    def keep_own(src, dst):
        at = pl.ds(pl.multiple_of(g * pack, pack), pack)
        dst[at, :] = src[at, :]

    ahead = near_copy(0, near_src, near_in, near_ssem, near_rsem, nxt)
    behind = near_copy(1, near_src, near_in, near_ssem, near_rsem, prv)
    each_peer(lambda o: far_copy(o, far_src, far_in, far_ssem, far_rsem).start())
    ahead.start()
    behind.start()
    keep_own(far_src, far_in)

    loads[1].wait()
    proj_own[:n_node, :] = mm(node_bf[...], wei[d:2 * d, :]).astype(BF16)
    proj_own[n_node:, :] = mm(node_bf[...], wei[2 * d:, :]).astype(BF16)
    first_near = n_node
    first_far = n_node + 2 * near
    far_cols = proj_ghost.shape[0] - 4 * near
    for e0 in range(0, n_edge, LANES):
        scol = column_of(snd_ref, e0, LANES)
        rcol = column_of(rcv_ref, e0, LANES)
        rows = slice(e0, e0 + LANES)
        lane_ids = iota((LANES, LANES), 1)
        for c0 in range(0, n_node, LANES):
            pick_own[rows, c0:c0 + LANES] = ones_where(scol == lane_ids + c0)
            pick_own[rows, n_node + c0:n_node + c0 + LANES] = ones_where(rcol == lane_ids + c0)
        for c0 in range(0, 2 * near, LANES):
            at = first_near + c0
            pick_ghost[rows, c0:c0 + LANES] = ones_where(scol == lane_ids + at)
            pick_ghost[rows, 2 * near + c0:2 * near + c0 + LANES] = ones_where(rcol == lane_ids + at)
        for c0 in range(0, far_cols, LANES):
            c = lane_ids + c0
            is_s = c < far_rows
            slot = jnp.where(is_s, scol, rcol)
            name = jnp.where(is_s, c, c - far_rows) + first_far
            pick_ghost[rows, 4 * near + c0:4 * near + c0 + LANES] = ones_where(slot == name)

    loads[2].wait()
    for e0 in range(0, n_edge, ROW_BLOCK):
        rows = slice(e0, e0 + ROW_BLOCK)
        pre[rows, :] = mm(edge_v[rows, :], wei[:d, :]) + mm(pick_own[rows, :], proj_own[...]) + ebi[...]

    rcv_row = rcv_ref[...]
    for r0, base, count in (
        (0, first_near, 2 * near), (2 * near, first_far, far_rows), (lent, 0, n_node)
    ):
        drop[r0:r0 + count, :] = ones_where(iota((count, n_edge), 0) + base == rcv_row)
    if far_cols > 2 * far_rows:
        proj_ghost[4 * near + 2 * far_rows:, :] = jnp.zeros((far_cols - 2 * far_rows, d), BF16)

    each_peer(lambda o: far_arrival(o, far_src, far_in, far_ssem, far_rsem).wait_recv())
    far_nodes = unpacked(far_in[...])
    proj_ghost[4 * near:4 * near + far_rows, :] = mm(far_nodes, wei[d:2 * d, :]).astype(BF16)
    proj_ghost[4 * near + far_rows:4 * near + 2 * far_rows, :] = mm(
        far_nodes, wei[2 * d:, :]
    ).astype(BF16)
    ahead.wait_recv()
    behind.wait_recv()
    proj_ghost[:2 * near, :] = mm(near_in[...], wei[d:2 * d, :]).astype(BF16)
    proj_ghost[2 * near:4 * near, :] = mm(near_in[...], wei[2 * d:, :]).astype(BF16)

    loads[3].wait()
    stores = []
    for i, e0 in enumerate(range(0, n_edge, ROW_BLOCK)):
        rows = slice(e0, e0 + ROW_BLOCK)
        hidden = silu(pre[rows, :] + mm(pick_ghost[rows, :], proj_ghost[...])).astype(BF16)
        message = norm_rows(mm(hidden, weo[...]) + ebo[...], egain[...], eshift[...])
        msg[rows, :] = message.astype(BF16)
        edge_v[rows, :] = (edge_v[rows, :].astype(F32) + message).astype(BF16)
        store = pltpu.make_async_copy(edge_v.at[rows], edge_out.at[rows], store_sem.at[i])
        store.start()
        stores.append(store)

    near_bsrc[...] = mm(drop[:2 * near, :], msg[...]).astype(BF16)
    back_prev = near_copy(0, near_bsrc, near_back, nback_ssem, nback_rsem, prv)
    back_next = near_copy(1, near_bsrc, near_back, nback_ssem, nback_rsem, nxt)
    back_prev.start()
    back_next.start()
    far_bsrc[...] = packed(mm(drop[2 * near:lent, :], msg[...]).astype(BF16))
    each_peer(lambda o: far_copy(o, far_bsrc, far_back, fback_ssem, fback_rsem).start())
    keep_own(far_bsrc, far_back)
    own_sum[...] = mm(drop[lent:, :], msg[...])

    loads[4].wait()
    loads[5].wait()
    node_pre = mm(node_bf[...], wni[:d, :]) + nbi[...]
    give = ones_where(iota((n_node, lent), 0) == lend_ref[:, :lent])

    each_peer(lambda o: far_arrival(o, far_bsrc, far_back, fback_ssem, fback_rsem).wait_recv())
    own_sum[...] += mm(give[:, 2 * near:], unpacked(far_back[...]))
    back_prev.wait_recv()
    back_next.wait_recv()
    lane_src[...] = (own_sum[...] + mm(give[:, :2 * near], near_back[...])).astype(BF16)
    swap = pltpu.make_async_remote_copy(
        src_ref=lane_src, dst_ref=lane_in, send_sem=lane_ssem, recv_sem=lane_rsem,
        device_id={"lane": other}, device_id_type=MESH,
    )
    swap.start()
    swap.wait_recv()
    summed = (lane_src[...].astype(F32) + lane_in[...].astype(F32)).astype(BF16)
    node_hidden = silu(node_pre + mm(summed, wni[d:, :])).astype(BF16)
    node_out[...] = node_v[...] + norm_rows(
        mm(node_hidden, wno[...]) + nbo[...], ngain[...], nshift[...]
    )

    ahead.wait_send()
    behind.wait_send()
    back_prev.wait_send()
    back_next.wait_send()
    swap.wait_send()
    each_peer(lambda o: far_copy(o, far_src, far_in, far_ssem, far_rsem).wait_send())
    each_peer(lambda o: far_copy(o, far_bsrc, far_back, fback_ssem, fback_rsem).wait_send())
    for store in stores:
        store.wait()


def per_device(
    node_latents, edge_latents, sender_slot, receiver_slot, near_send, far_send,
    w_edge_in, w_edge_out, w_node_in, w_node_out,
    edge_bias_in, edge_bias_out, edge_gain, edge_shift,
    node_bias_in, node_bias_out, node_gain, node_shift,
):
    n_node, d = node_latents.shape
    n_edge = edge_latents.shape[0]
    near = near_send.shape[2]
    peers, far = far_send.shape[1:]
    n_patch, n_sub, n_lane = (lax.axis_size(a) for a in ("patch", "sub", "lane"))
    far_rows = peers * far
    lent = 2 * near + far_rows
    lent_pad = -(-lent // LANES) * LANES
    ghost_k = 4 * near + -(-2 * far_rows // LANES) * LANES
    pack = far * (d // LANES)
    blocks = n_edge // ROW_BLOCK
    lend = jnp.concatenate(
        [near_send.reshape(1, -1), far_send.reshape(1, -1),
         jnp.zeros((1, lent_pad - lent), jnp.int32)], axis=1
    )
    vectors = [v.reshape(1, d) for v in (
        edge_bias_in, edge_bias_out, edge_gain, edge_shift,
        node_bias_in, node_bias_out, node_gain, node_shift)]
    hbm = pl.BlockSpec(memory_space=pl.ANY)
    vmem = pl.BlockSpec(memory_space=pltpu.VMEM)
    dma = pltpu.SemaphoreType.DMA
    far_shape = (peers * pack, LANES)
    macs = n_edge * d * (3 * d + ghost_k + lent + n_node) + n_node * d * 6 * d
    return tuple(pl.pallas_call(
        functools.partial(layer_kernel, (n_patch, n_sub, n_lane, near, far)),
        out_shape=(
            jax.ShapeDtypeStruct((n_node, d), F32),
            jax.ShapeDtypeStruct((n_edge, d), BF16),
        ),
        in_specs=[hbm] * 6 + [vmem] * (3 + len(vectors)),
        out_specs=(vmem, hbm),
        scratch_shapes=[
            pltpu.VMEM((n_node, d), F32),
            pltpu.VMEM((n_edge, d), BF16),
            pltpu.VMEM(w_edge_in.shape, BF16),
            pltpu.VMEM(w_edge_out.shape, BF16),
            pltpu.VMEM(w_node_in.shape, BF16),
            pltpu.VMEM(w_node_out.shape, BF16),
            pltpu.VMEM((n_node, d), BF16),
            pltpu.VMEM((lent_pad, n_node), BF16),
            pltpu.VMEM((2 * near, d), BF16),
            pltpu.VMEM(far_shape, BF16),
            pltpu.VMEM((2 * near, d), BF16),
            pltpu.VMEM(far_shape, BF16),
            pltpu.VMEM((n_edge, 2 * n_node), BF16),
            pltpu.VMEM((n_edge, ghost_k), BF16),
            pltpu.VMEM((2 * n_node, d), BF16),
            pltpu.VMEM((ghost_k, d), BF16),
            pltpu.VMEM((lent + n_node, n_edge), BF16),
            pltpu.VMEM((n_edge, d), F32),
            pltpu.VMEM((n_edge, d), BF16),
            pltpu.VMEM((2 * near, d), BF16),
            pltpu.VMEM(far_shape, BF16),
            pltpu.VMEM((2 * near, d), BF16),
            pltpu.VMEM(far_shape, BF16),
            pltpu.VMEM((n_node, d), BF16),
            pltpu.VMEM((n_node, d), BF16),
            pltpu.VMEM((n_node, d), F32),
            dma((6,)), dma((blocks,)),
            dma((2,)), dma((2,)), dma((peers,)), dma((peers,)),
            dma((2,)), dma((2,)), dma((peers,)), dma((peers,)),
            dma, dma,
        ],
        compiler_params=pltpu.CompilerParams(
            collective_id=0, has_side_effects=True, vmem_limit_bytes=(48 if peers <= 16 else 60) * 1024 * 1024
        ),
        cost_estimate=pl.CostEstimate(
            flops=2 * macs, bytes_accessed=8 * 1024 * 1024, transcendentals=n_edge * d
        ),
        name="mesh_layer",
    )(
        node_latents, edge_latents, w_edge_in, w_edge_out, w_node_in, w_node_out,
        sender_slot.reshape(1, n_edge), receiver_slot.reshape(1, n_edge), lend, *vectors,
    ))


def solution(mesh):
    nodes = P(("groups", "patch", "sub"), None)
    edges = P(("groups", "patch", "sub", "lane"), None)
    per_edge = P(("groups", "patch", "sub", "lane"))
    lists = P(("groups", "patch", "sub", "lane"), None, None)
    in_specs = (nodes, edges, per_edge, per_edge, lists, lists) + (P(),) * 12
    return jax.shard_map(
        per_device, mesh=mesh, in_specs=in_specs, out_specs=(nodes, edges), check_vma=False
    )
```

time: 78.2 us -> 46.5 us (0.59)
  Pallas kernels: 0 us -> 29.5 us
  other arithmetic: 16.1 us -> 0.69 us
  starting transfers between devices: 13.5 us -> 0 us
  matrix products: 9.65 us -> 0 us
  blocking collectives: 8.68 us -> 0 us
  waiting for transfers between devices: 7.24 us -> 0 us
  local copies, waits for them, and re-layouts: 21.4 us -> 15.1 us
    pallas_call x0 -> x1, Pallas kernels: none -> 29.5 us  [per_device(): pl.pallas_call(functools.partial(layer_kernel, (n_patch, n_sub, n_lane, n...]
    gather x6 -> x0, local copies, waits for them, and re-layouts: 13.1 us -> none  [the longest x1 5.08 us: per_device(): ghost_send[sender_slot].astype(jnp.float32)]
    unnamed x41 -> x33, local copies, waits for them, and re-layouts: 3.65 us -> 14.9 us
    scatter-add x2 -> x0, other arithmetic: 10.1 us -> none  [the longest x1 7.52 us: per_device(): jax.ops.segment_sum(message, receiver_slot, num_segments=ghost.shape[0])]
    dot_general x5 -> x0, matrix products: 9.65 us -> none  [the longest x1 3.65 us: per_device(): jnp.dot(hidden, w_edge_out, preferred_element_type=jnp.float32)]
    psum x1 -> x0, blocking collectives: 8.68 us -> none  [per_device(): summed_all = lax.psum(summed, 'lane')]
    all_to_all x2 -> x0, starting transfers between devices: 7.79 us -> none  [the longest x1 4.14 us: per_device(): lax.all_to_all(far_sums, ('patch', 'sub'), split_axis=0, concat_axis=0, t...]
    all_to_all x2 -> x0, waiting for transfers between devices: 7.23 us -> none  [the longest x1 4.15 us: per_device(): lax.all_to_all(far_sums, ('patch', 'sub'), split_axis=0, concat_axis=0, t...]
  transfers between devices with their start and end apart: 6 -> 0, of which waited for: 2 -> 0; matrix products, arithmetic and copies ran while one was open for 9% -> 0% of each run, Pallas kernels for 0% -> 0%
where the time goes in v1:
time: 46.5 us; the launch traced here: 45.9 us
  Pallas kernels  29.5 us (63%)
  local copies, waits for them, and re-layouts  15.1 us (32%)
  other arithmetic  0.69 us (1%)
  between operations  0.66 us (1%)
    pallas_call x1, Pallas kernels, per_device(): pl.pallas_call(functools.partial(layer_kernel, (n_patch, n_sub, n_lane, n...  29.5 us
    unnamed x33, local copies, waits for them, and re-layouts  14.9 us

profile of v1, /device:TPU:1, one launch (start us, length us, event | category | flops | bytes accessed | tf_op | source)
XLA Modules:
  0.0 45.9 jit_solution(16698086979299467774)
XLA Ops:
  0.6 0.1 pad.2.clone
  0.7 0.8 %copy.21 = s32[1,8,4]{2,1,0:T(8,128)S(1)} copy(s32[1,8,4]{1,2,0:T(4,128)} %param.23) | data formatting | bytes 256 | tf_op args[5]
  1.5 0.1 reshape.43
  1.6 0.7 %reshape_add_fusion.lend_ref = s32[1,384]{1,0:T(1,128)S(1)} fusion(s32[384]{0:T(512)S(1)} %pad.2.clone, s32[1,32]{1,0:T(1,128)S(1)} %reshape.43, s32[1,256]{1,0:T(1,128)} %bitcast.21), kind=kLoop, calls=%fused_computation | loop fusion | flops 768 | bytes 4224 | tf_op jit(solution)/shard_map/concatenate | solution.py:309
  2.2 0.0 copy-start
  2.2 1.2 %copy-done = bf16[1024,512]{1,0:T(8,128)(2,1)S(1)} copy-done((bf16[1024,512]{1,0:T(8,128)(2,1)S(1)}, bf16[1024,512]{1,0:T(8,128)(2,1)}, u32[]{:S(2)}) %copy-start) | copy-done | bytes 1048600
  3.5 0.0 copy-start.1
  3.5 1.2 %copy-done.1 = bf16[1024,512]{1,0:T(8,128)(2,1)S(1)} copy-done((bf16[1024,512]{1,0:T(8,128)(2,1)S(1)}, bf16[1024,512]{1,0:T(8,128)(2,1)}, u32[]{:S(2)}) %copy-start.1) | copy-done | bytes 1048600
  4.7 1.0 %copy-done.2 = f32[256,512]{1,0:T(8,128)S(1)} copy-done((f32[256,512]{1,0:T(8,128)S(1)}, f32[256,512]{1,0:T(8,128)}, u32[]{:S(2)}) %copy-start.2) | copy-done | bytes 524312
  5.7 1.0 %copy-done.3 = bf16[512,512]{1,0:T(8,128)(2,1)S(1)} copy-done((bf16[512,512]{1,0:T(8,128)(2,1)S(1)}, bf16[512,512]{1,0:T(8,128)(2,1)}, u32[]{:S(2)}) %copy-start.3) | copy-done | bytes 524312
  6.8 1.0 %copy-done.4 = bf16[512,512]{1,0:T(8,128)(2,1)S(1)} copy-done((bf16[512,512]{1,0:T(8,128)(2,1)S(1)}, bf16[512,512]{1,0:T(8,128)(2,1)}, u32[]{:S(2)}) %copy-start.4) | copy-done | bytes 524312
  7.8 0.7 %copy-done.5 = s32[1024]{0:T(1024)S(1)} copy-done((s32[1024]{0:T(1024)S(1)}, s32[1024]{0:T(1024)}, u32[]{:S(2)}) %copy-start.5) | copy-done | bytes 4120
  8.5 0.7 %copy-done.6 = s32[1024]{0:T(1024)S(1)} copy-done((s32[1024]{0:T(1024)S(1)}, s32[1024]{0:T(1024)}, u32[]{:S(2)}) %copy-start.6) | copy-done | bytes 4120
  9.2 0.7 %copy-done.7 = f32[512]{0:T(512)S(1)} copy-done((f32[512]{0:T(512)S(1)}, f32[512]{0:T(512)}, u32[]{:S(2)}) %copy-start.7) | copy-done | bytes 2072
  9.9 0.7 %copy-done.8 = f32[512]{0:T(512)S(1)} copy-done((f32[512]{0:T(512)S(1)}, f32[512]{0:T(512)}, u32[]{:S(2)}) %copy-start.8) | copy-done | bytes 2072
  10.6 0.7 %copy-done.9 = f32[512]{0:T(512)S(1)} copy-done((f32[512]{0:T(512)S(1)}, f32[512]{0:T(512)}, u32[]{:S(2)}) %copy-start.9) | copy-done | bytes 2072
  11.2 0.7 %copy-done.10 = f32[512]{0:T(512)S(1)} copy-done((f32[512]{0:T(512)S(1)}, f32[512]{0:T(512)}, u32[]{:S(2)}) %copy-start.10) | copy-done | bytes 2072
  11.9 0.7 %copy-done.11 = f32[512]{0:T(512)S(1)} copy-done((f32[512]{0:T(512)S(1)}, f32[512]{0:T(512)}, u32[]{:S(2)}) %copy-start.11) | copy-done | bytes 2072
  12.6 0.7 %copy-done.12 = f32[512]{0:T(512)S(1)} copy-done((f32[512]{0:T(512)S(1)}, f32[512]{0:T(512)}, u32[]{:S(2)}) %copy-start.12) | copy-done | bytes 2072
  13.3 0.7 %copy-done.13 = f32[512]{0:T(512)S(1)} copy-done((f32[512]{0:T(512)S(1)}, f32[512]{0:T(512)}, u32[]{:S(2)}) %copy-start.13) | copy-done | bytes 2072
  14.0 0.7 %copy-done.14 = f32[512]{0:T(512)S(1)} copy-done((f32[512]{0:T(512)S(1)}, f32[512]{0:T(512)}, u32[]{:S(2)}) %copy-start.14) | copy-done | bytes 2072
  14.6 29.5 %mesh_layer.1 = (f32[256,512]{1,0:T(8,128)S(1)}, bf16[1024,512]{1,0:T(8,128)(2,1)S(1)}) custom-call(f32[256,512]{1,0:T(8,128)S(1)} %copy-done.2, bf16[1024,512]{1,0:T(8,128)(2,1)S(1)} %copy-done, bf16[1536,512]{1,0:T(8,128)(2,1)} %wei_hbm.1, bf16[512,512]{1,0:T(8,128)(2,1)S(1)} %copy-done.3, bf16[1024,512]{1,0:T(8,128)(2,1)S(1)} %copy-done.1, ...), custom_call_target="tpu_custom_call" | custom-call | flops 3657433088 | bytes 8388608 | tf_op jit(solution)/shard_map/mesh_layer/pallas_call | solution.py:321
  44.1 0.8 %copy.24 = f32[256,512]{1,0:T(8,128)} copy(f32[256,512]{1,0:T(8,128)S(1)} %get-tuple-element.4) | data formatting | bytes 1048576
  44.9 1.0 %copy.25 = bf16[1024,512]{1,0:T(8,128)(2,1)} copy(bf16[1024,512]{1,0:T(8,128)(2,1)S(1)} %get-tuple-element.5) | data formatting | bytes 2097152
  (14 shorter events, 0.0 us)
Async XLA Ops:
  2.2 1.2 %copy-start = (bf16[1024,512]{1,0:T(8,128)(2,1)S(1)}, bf16[1024,512]{1,0:T(8,128)(2,1)}, u32[]{:S(2)}) copy-start(bf16[1024,512]{1,0:T(8,128)(2,1)} %edge_hbm.1) | copy-start | bytes 3145732
  3.5 1.2 %copy-start.1 = (bf16[1024,512]{1,0:T(8,128)(2,1)S(1)}, bf16[1024,512]{1,0:T(8,128)(2,1)}, u32[]{:S(2)}) copy-start(bf16[1024,512]{1,0:T(8,128)(2,1)} %wni_hbm.1) | copy-start | bytes 3145732
  4.7 1.0 %copy-start.2 = (f32[256,512]{1,0:T(8,128)S(1)}, f32[256,512]{1,0:T(8,128)}, u32[]{:S(2)}) copy-start(f32[256,512]{1,0:T(8,128)} %node_hbm.1) | copy-start | bytes 1572868
  5.7 1.0 %copy-start.3 = (bf16[512,512]{1,0:T(8,128)(2,1)S(1)}, bf16[512,512]{1,0:T(8,128)(2,1)}, u32[]{:S(2)}) copy-start(bf16[512,512]{1,0:T(8,128)(2,1)} %weo_hbm.1) | copy-start | bytes 1572868
  6.8 1.0 %copy-start.4 = (bf16[512,512]{1,0:T(8,128)(2,1)S(1)}, bf16[512,512]{1,0:T(8,128)(2,1)}, u32[]{:S(2)}) copy-start(bf16[512,512]{1,0:T(8,128)(2,1)} %wno_hbm.1) | copy-start | bytes 1572868
  7.8 0.7 %copy-start.5 = (s32[1024]{0:T(1024)S(1)}, s32[1024]{0:T(1024)}, u32[]{:S(2)}) copy-start(s32[1024]{0:T(1024)} %param.20) | copy-start | bytes 12292
  8.5 0.7 %copy-start.6 = (s32[1024]{0:T(1024)S(1)}, s32[1024]{0:T(1024)}, u32[]{:S(2)}) copy-start(s32[1024]{0:T(1024)} %param.21) | copy-start | bytes 12292
  9.2 0.7 %copy-start.7 = (f32[512]{0:T(512)S(1)}, f32[512]{0:T(512)}, u32[]{:S(2)}) copy-start(f32[512]{0:T(512)} %param.28) | copy-start | bytes 6148
  9.9 0.7 %copy-start.8 = (f32[512]{0:T(512)S(1)}, f32[512]{0:T(512)}, u32[]{:S(2)}) copy-start(f32[512]{0:T(512)} %param.29) | copy-start | bytes 6148
  10.6 0.7 %copy-start.9 = (f32[512]{0:T(512)S(1)}, f32[512]{0:T(512)}, u32[]{:S(2)}) copy-start(f32[512]{0:T(512)} %param.30) | copy-start | bytes 6148
  11.2 0.7 %copy-start.10 = (f32[512]{0:T(512)S(1)}, f32[512]{0:T(512)}, u32[]{:S(2)}) copy-start(f32[512]{0:T(512)} %param.31) | copy-start | bytes 6148
  11.9 0.7 %copy-start.11 = (f32[512]{0:T(512)S(1)}, f32[512]{0:T(512)}, u32[]{:S(2)}) copy-start(f32[512]{0:T(512)} %param.32) | copy-start | bytes 6148
  12.6 0.7 %copy-start.12 = (f32[512]{0:T(512)S(1)}, f32[512]{0:T(512)}, u32[]{:S(2)}) copy-start(f32[512]{0:T(512)} %param.33) | copy-start | bytes 6148
  13.3 0.7 %copy-start.13 = (f32[512]{0:T(512)S(1)}, f32[512]{0:T(512)}, u32[]{:S(2)}) copy-start(f32[512]{0:T(512)} %param.34) | copy-start | bytes 6148
  14.0 0.7 %copy-start.14 = (f32[512]{0:T(512)S(1)}, f32[512]{0:T(512)}, u32[]{:S(2)}) copy-start(f32[512]{0:T(512)} %param.35) | copy-start | bytes 6148

commit v2 on v1

--- a/solution.py
+++ b/solution.py
@@ -41,14 +41,24 @@
 def layer_kernel(
     dims,
     node_hbm, edge_hbm, wei_hbm, weo_hbm, wni_hbm, wno_hbm,
-    snd_ref, rcv_ref, lend_ref,
-    ebi, ebo, egain, eshift, nbi, nbo, ngain, nshift,
+    snd_hbm, rcv_hbm, near_hbm, far_hbm, *rest,
+):
+    vec_hbm, rest = rest[:8], rest[8:]
+    layer_body(
+        dims, (node_hbm, wei_hbm, edge_hbm, weo_hbm, wni_hbm, wno_hbm),
+        (snd_hbm, rcv_hbm, near_hbm, far_hbm), vec_hbm, *rest
+    )
+
+
+def layer_body(
+    dims, big_hbm, index_hbm, vec_hbm,
     node_out, edge_out,
+    snd_ref, rcv_ref, near_idx, far_idx, lend_ref, vecs,
     node_v, edge_v, wei, weo, wni, wno, node_bf,
     lend_sel, near_src, far_src, near_in, far_in,
     pick_own, pick_ghost, proj_own, proj_ghost, drop, pre, msg,
     near_bsrc, far_bsrc, near_back, far_back, lane_src, lane_in, own_sum,
-    load_sem, store_sem, near_ssem, near_rsem, far_ssem, far_rsem,
+    load_sem, index_sem, vec_sem, store_sem, near_ssem, near_rsem, far_ssem, far_rsem,
     nback_ssem, nback_rsem, fback_ssem, fback_rsem, lane_ssem, lane_rsem,
 ):
     n_patch, n_sub, n_lane, near, far = dims
@@ -59,15 +69,19 @@
     n_edge = edge_v.shape[0]
     col_parts = d // LANES
 
-    loads = [
-        pltpu.make_async_copy(src, dst, load_sem.at[i])
-        for i, (src, dst) in enumerate(
-            [(node_hbm, node_v), (wei_hbm, wei), (edge_hbm, edge_v),
-             (weo_hbm, weo), (wni_hbm, wni), (wno_hbm, wno)]
-        )
-    ]
-    for load in loads:
-        load.start()
+    def fetch(sources, targets, sems):
+        copies = [
+            pltpu.make_async_copy(src, dst, sems.at[i])
+            for i, (src, dst) in enumerate(zip(sources, targets))
+        ]
+        for copy in copies:
+            copy.start()
+        return copies
+
+    indices = fetch(index_hbm[::-1], (far_idx, near_idx, rcv_ref, snd_ref), index_sem)
+    loads = fetch(big_hbm, (node_v, wei, edge_v, weo, wni, wno), load_sem)
+    vec_loads = fetch(vec_hbm, [vecs.at[i] for i in range(8)], vec_sem)
+    ebi, ebo, egain, eshift, nbi, nbo, ngain, nshift = (vecs.at[i] for i in range(8))
 
     p = lax.axis_index("patch")
     s = lax.axis_index("sub")
@@ -105,6 +119,15 @@
         return jnp.transpose(jnp.broadcast_to(row, (LANES, width)))
 
     lent = 2 * near + far_rows
+    indices[0].wait()
+    indices[1].wait()
+    lend_ref[...] = jnp.zeros(lend_ref.shape, jnp.int32)
+    lend_ref[:, :2 * near] = near_idx[...]
+    spread = jnp.zeros((peers, far_rows), jnp.int32)
+    for k in range(far):
+        here = iota((peers, far_rows), 1) == iota((peers, far_rows), 0) * far + k
+        spread = jnp.where(here, far_idx[:, k:k + 1], spread)
+    lend_ref[:, 2 * near:lent] = jnp.sum(spread, axis=0, keepdims=True)
     for r0 in range(0, lent, LANES):
         col = column_of(lend_ref, r0, LANES)
         for c0 in range(0, n_node, LANES):
@@ -184,6 +207,11 @@
     ahead.start()
     behind.start()
     keep_own(far_src, far_in)
+
+    indices[2].wait()
+    indices[3].wait()
+    for load in vec_loads:
+        load.wait()
 
     loads[1].wait()
     proj_own[:n_node, :] = mm(node_bf[...], wei[d:2 * d, :]).astype(BF16)
@@ -306,14 +334,10 @@
     ghost_k = 4 * near + -(-2 * far_rows // LANES) * LANES
     pack = far * (d // LANES)
     blocks = n_edge // ROW_BLOCK
-    lend = jnp.concatenate(
-        [near_send.reshape(1, -1), far_send.reshape(1, -1),
-         jnp.zeros((1, lent_pad - lent), jnp.int32)], axis=1
-    )
     vectors = [v.reshape(1, d) for v in (
         edge_bias_in, edge_bias_out, edge_gain, edge_shift,
         node_bias_in, node_bias_out, node_gain, node_shift)]
-    hbm = pl.BlockSpec(memory_space=pl.ANY)
+    hbm = pl.BlockSpec(memory_space=pltpu.HBM)
     vmem = pl.BlockSpec(memory_space=pltpu.VMEM)
     dma = pltpu.SemaphoreType.DMA
     far_shape = (peers * pack, LANES)
@@ -324,9 +348,15 @@
             jax.ShapeDtypeStruct((n_node, d), F32),
             jax.ShapeDtypeStruct((n_edge, d), BF16),
         ),
-        in_specs=[hbm] * 6 + [vmem] * (3 + len(vectors)),
+        in_specs=[hbm] * (10 + len(vectors)),
         out_specs=(vmem, hbm),
         scratch_shapes=[
+            pltpu.VMEM((1, n_edge), jnp.int32),
+            pltpu.VMEM((1, n_edge), jnp.int32),
+            pltpu.VMEM((1, 2 * near), jnp.int32),
+            pltpu.VMEM((peers, far), jnp.int32),
+            pltpu.VMEM((1, lent_pad), jnp.int32),
+            pltpu.VMEM((len(vectors), 1, d), F32),
             pltpu.VMEM((n_node, d), F32),
             pltpu.VMEM((n_edge, d), BF16),
             pltpu.VMEM(w_edge_in.shape, BF16),
@@ -353,13 +383,13 @@
             pltpu.VMEM((n_node, d), BF16),
             pltpu.VMEM((n_node, d), BF16),
             pltpu.VMEM((n_node, d), F32),
-            dma((6,)), dma((blocks,)),
+            dma((6,)), dma((4,)), dma((len(vectors),)), dma((blocks,)),
             dma((2,)), dma((2,)), dma((peers,)), dma((peers,)),
             dma((2,)), dma((2,)), dma((peers,)), dma((peers,)),
             dma, dma,
         ],
         compiler_params=pltpu.CompilerParams(
-            collective_id=0, has_side_effects=True, vmem_limit_bytes=(48 if peers <= 16 else 60) * 1024 * 1024
+            collective_id=0, has_side_effects=True, vmem_limit_bytes=62 * 1024 * 1024
         ),
         cost_estimate=pl.CostEstimate(
             flops=2 * macs, bytes_accessed=8 * 1024 * 1024, transcendentals=n_edge * d
@@ -367,7 +397,8 @@
         name="mesh_layer",
     )(
         node_latents, edge_latents, w_edge_in, w_edge_out, w_node_in, w_node_out,
-        sender_slot.reshape(1, n_edge), receiver_slot.reshape(1, n_edge), lend, *vectors,
+        sender_slot.reshape(1, n_edge), receiver_slot.reshape(1, n_edge),
+        near_send.reshape(1, 2 * near), far_send.reshape(peers, far), *vectors,
     ))
 
 

time: 46.5 us -> 34.3 us (0.74)
  local copies, waits for them, and re-layouts: 15.1 us -> 4.28 us
  other arithmetic: 0.69 us -> 0 us
    unnamed x33 -> x4, local copies, waits for them, and re-layouts: 14.9 us -> 2.93 us
    reshape x1, local copies, waits for them, and re-layouts: 0.08 us -> 1.35 us  [per_device(): far_send.reshape(peers, far)]
    concatenate x1 -> x0, other arithmetic: 0.69 us -> none  [per_device(): jnp.concatenate([near_send.reshape(1, -1), far_send.reshape(1, -1), jnp.z...]
where the time goes in v2:
time: 34.3 us; the launch traced here: 34.1 us
  Pallas kernels  29.2 us (85%)
  local copies, waits for them, and re-layouts  4.28 us (12%)
  between operations  0.65 us (2%)
    pallas_call x1, Pallas kernels, per_device(): pl.pallas_call(functools.partial(layer_kernel, (n_patch, n_sub, n_lane, n...  29.2 us
    unnamed x4, local copies, waits for them, and re-layouts  2.93 us
    reshape x1, local copies, waits for them, and re-layouts, per_device(): far_send.reshape(peers, far)  1.35 us

profile of v2, /device:TPU:1, one launch (start us, length us, event | category | flops | bytes accessed | tf_op | source)
XLA Modules:
  0.0 34.1 jit_solution(5864819081664706281)
XLA Ops:
  0.6 1.3 %copy.20.far_hbm = s32[8,4]{1,0:T(8,128)} copy(s32[8,4]{0,1:T(4,128)} %bitcast.12) | data formatting | bytes 256 | tf_op jit(solution)/shard_map/reshape | solution.py:401
  2.0 29.2 %mesh_layer.1 = (f32[256,512]{1,0:T(8,128)}, bf16[1024,512]{1,0:T(8,128)(2,1)}) custom-call(f32[256,512]{1,0:T(8,128)} %node_hbm.1, bf16[1024,512]{1,0:T(8,128)(2,1)} %edge_hbm.1, bf16[1536,512]{1,0:T(8,128)(2,1)} %wei_hbm.1, bf16[512,512]{1,0:T(8,128)(2,1)} %weo_hbm.1, bf16[1024,512]{1,0:T(8,128)(2,1)} %wni_hbm.1, bf16[512,512]{1,0:T(8,128)(2,1)} %wno_hbm.1, ...), custom_call_target="tpu_custom_call" | custom-call | flops 3657433088 | bytes 8388608 | tf_op jit(solution)/shard_map/mesh_layer/pallas_call | solution.py:345
  31.1 0.0 copy-start
  31.2 2.0 %copy.23 = f32[256,512]{1,0:T(8,128)} copy(f32[256,512]{1,0:T(8,128)} %get-tuple-element.4) | data formatting | bytes 1048576
  33.1 0.0 copy-done
  33.1 1.0 %copy.24 = bf16[1024,512]{1,0:T(8,128)(2,1)} copy(bf16[1024,512]{1,0:T(8,128)(2,1)S(1)} %copy-done) | data formatting | bytes 2097152
Async XLA Ops:
  31.1 2.0 %copy-start = (bf16[1024,512]{1,0:T(8,128)(2,1)S(1)}, bf16[1024,512]{1,0:T(8,128)(2,1)}, u32[]{:S(2)}) copy-start(bf16[1024,512]{1,0:T(8,128)(2,1)} %get-tuple-element.5) | copy-start | bytes 3145732

commit v3 on v2

--- a/solution.py
+++ b/solution.py
@@ -12,6 +12,7 @@
 BF16 = jnp.bfloat16
 LANES = 128
 ROW_BLOCK = 256
+PIECES = 4
 
 
 def mm(a, b):
@@ -123,11 +124,9 @@
     indices[1].wait()
     lend_ref[...] = jnp.zeros(lend_ref.shape, jnp.int32)
     lend_ref[:, :2 * near] = near_idx[...]
-    spread = jnp.zeros((peers, far_rows), jnp.int32)
     for k in range(far):
-        here = iota((peers, far_rows), 1) == iota((peers, far_rows), 0) * far + k
-        spread = jnp.where(here, far_idx[:, k:k + 1], spread)
-    lend_ref[:, 2 * near:lent] = jnp.sum(spread, axis=0, keepdims=True)
+        at = 2 * near + k * peers
+        lend_ref[:, at:at + peers] = far_idx[k:k + 1, :]
     for r0 in range(0, lent, LANES):
         col = column_of(lend_ref, r0, LANES)
         for c0 in range(0, n_node, LANES):
@@ -138,12 +137,12 @@
     def packer(j):
         r = iota((peers * pack, far_rows), 0)
         c = iota((peers * pack, far_rows), 1)
-        return ones_where(r == c // far * pack + j * far + c % far)
+        return ones_where(r == c % peers * pack + j * far + c // peers)
 
     def unpacker(j):
         r = iota((far_rows, peers * pack), 0)
         c = iota((far_rows, peers * pack), 1)
-        return ones_where(c == r // far * pack + j * far + r % far)
+        return ones_where(c == r % peers * pack + j * far + r // peers)
 
     def packed(rows):
         total = mm(packer(0), rows[:, :LANES])
@@ -159,9 +158,6 @@
     loads[0].wait()
     node_bf[...] = node_v[...].astype(BF16)
     near_src[...] = mm(lend_sel[:2 * near, :], node_bf[...]).astype(BF16)
-    far_src[...] = packed(
-        mm(lend_sel[2 * near:lent, :], node_bf[...]).astype(BF16)
-    )
 
     pl.semaphore_wait(barrier, peers)
 
@@ -203,9 +199,12 @@
 
     ahead = near_copy(0, near_src, near_in, near_ssem, near_rsem, nxt)
     behind = near_copy(1, near_src, near_in, near_ssem, near_rsem, prv)
-    each_peer(lambda o: far_copy(o, far_src, far_in, far_ssem, far_rsem).start())
     ahead.start()
     behind.start()
+    far_src[...] = packed(
+        mm(lend_sel[2 * near:lent, :], node_bf[...]).astype(BF16)
+    )
+    each_peer(lambda o: far_copy(o, far_src, far_in, far_ssem, far_rsem).start())
     keep_own(far_src, far_in)
 
     indices[2].wait()
@@ -235,7 +234,8 @@
             c = lane_ids + c0
             is_s = c < far_rows
             slot = jnp.where(is_s, scol, rcol)
-            name = jnp.where(is_s, c, c - far_rows) + first_far
+            row = jnp.where(is_s, c, c - far_rows)
+            name = first_far + row % peers * far + row // peers
             pick_ghost[rows, 4 * near + c0:4 * near + c0 + LANES] = ones_where(slot == name)
 
     loads[2].wait()
@@ -244,10 +244,10 @@
         pre[rows, :] = mm(edge_v[rows, :], wei[:d, :]) + mm(pick_own[rows, :], proj_own[...]) + ebi[...]
 
     rcv_row = rcv_ref[...]
-    for r0, base, count in (
-        (0, first_near, 2 * near), (2 * near, first_far, far_rows), (lent, 0, n_node)
-    ):
+    for r0, base, count in ((0, first_near, 2 * near), (lent, 0, n_node)):
         drop[r0:r0 + count, :] = ones_where(iota((count, n_edge), 0) + base == rcv_row)
+    row = iota((far_rows, n_edge), 0)
+    drop[2 * near:lent, :] = ones_where(first_far + row % peers * far + row // peers == rcv_row)
     if far_cols > 2 * far_rows:
         proj_ghost[4 * near + 2 * far_rows:, :] = jnp.zeros((far_cols - 2 * far_rows, d), BF16)
 
@@ -315,6 +315,21 @@
     each_peer(lambda o: far_copy(o, far_bsrc, far_back, fback_ssem, fback_rsem).wait_send())
     for store in stores:
         store.wait()
+
+
+def hand_over(node_in, edge_in, node_out, edge_out, sems):
+    copies = []
+    for a, (src, dst) in enumerate(((edge_in, edge_out), (node_in, node_out))):
+        step = src.shape[0] // PIECES
+        for i in range(PIECES):
+            rows = pl.ds(i * step, step)
+            copies.append(pltpu.make_async_copy(
+                src.at[rows], dst.at[rows], sems.at[a * PIECES + i]
+            ))
+    for copy in copies:
+        copy.start()
+    for copy in copies:
+        copy.wait()
 
 
 def per_device(
@@ -342,7 +357,7 @@
     dma = pltpu.SemaphoreType.DMA
     far_shape = (peers * pack, LANES)
     macs = n_edge * d * (3 * d + ghost_k + lent + n_node) + n_node * d * 6 * d
-    return tuple(pl.pallas_call(
+    results = pl.pallas_call(
         functools.partial(layer_kernel, (n_patch, n_sub, n_lane, near, far)),
         out_shape=(
             jax.ShapeDtypeStruct((n_node, d), F32),
@@ -354,7 +369,7 @@
             pltpu.VMEM((1, n_edge), jnp.int32),
             pltpu.VMEM((1, n_edge), jnp.int32),
             pltpu.VMEM((1, 2 * near), jnp.int32),
-            pltpu.VMEM((peers, far), jnp.int32),
+            pltpu.VMEM((far, peers), jnp.int32),
             pltpu.VMEM((1, lent_pad), jnp.int32),
             pltpu.VMEM((len(vectors), 1, d), F32),
             pltpu.VMEM((n_node, d), F32),
@@ -398,8 +413,17 @@
     )(
         node_latents, edge_latents, w_edge_in, w_edge_out, w_node_in, w_node_out,
         sender_slot.reshape(1, n_edge), receiver_slot.reshape(1, n_edge),
-        near_send.reshape(1, 2 * near), far_send.reshape(peers, far), *vectors,
-    ))
+        near_send.reshape(1, 2 * near), jnp.swapaxes(far_send, 1, 2).reshape(far, peers), *vectors,
+    )
+    return tuple(pl.pallas_call(
+        hand_over,
+        out_shape=tuple(jax.ShapeDtypeStruct(r.shape, r.dtype) for r in results),
+        in_specs=[hbm] * 2,
+        out_specs=(hbm, hbm),
+        scratch_shapes=[dma((2 * PIECES,))],
+        compiler_params=pltpu.CompilerParams(vmem_limit_bytes=62 * 1024 * 1024),
+        name="hand_over",
+    )(*results))
 
 
 def solution(mesh):

time: 34.3 us -> 79.8 us (2.33)
  Pallas kernels: 29.2 us -> 79 us
  local copies, waits for them, and re-layouts: 4.28 us -> 0 us
    pallas_call x0 -> x1, Pallas kernels: none -> 48.8 us  [per_device(): pl.pallas_call(hand_over, out_shape=tuple((jax.ShapeDtypeStruct(r.shape,...]
    unnamed x4 -> x0, local copies, waits for them, and re-layouts: 2.93 us -> none
    reshape x1 -> x0, local copies, waits for them, and re-layouts: 1.35 us -> none  [per_device(): far_send.reshape(peers, far)]
    pallas_call x1, Pallas kernels: 29.2 us -> 30.2 us  [per_device(): pl.pallas_call(functools.partial(layer_kernel, (n_patch, n_sub, n_lane, n...]
where the time goes in v3:
time: 79.8 us; the launch traced here: 79.7 us
  Pallas kernels  79 us (99%)
    pallas_call x1, Pallas kernels, per_device(): pl.pallas_call(hand_over, out_shape=tuple((jax.ShapeDtypeStruct(r.shape,...  48.8 us
    pallas_call x1, Pallas kernels, per_device(): pl.pallas_call(functools.partial(layer_kernel, (n_patch, n_sub, n_lane, n...  30.2 us

profile of v3, /device:TPU:1, one launch (start us, length us, event | category | flops | bytes accessed | tf_op | source)
XLA Modules:
  0.0 79.7 jit_solution(11820867035940937774)
XLA Ops:
  0.6 30.2 %mesh_layer.1 = (f32[256,512]{1,0:T(8,128)}, bf16[1024,512]{1,0:T(8,128)(2,1)}) custom-call(f32[256,512]{1,0:T(8,128)} %node_hbm.1, bf16[1024,512]{1,0:T(8,128)(2,1)} %edge_hbm.1, bf16[1536,512]{1,0:T(8,128)(2,1)} %wei_hbm.1, bf16[512,512]{1,0:T(8,128)(2,1)} %weo_hbm.1, bf16[1024,512]{1,0:T(8,128)(2,1)} %wni_hbm.1, bf16[512,512]{1,0:T(8,128)(2,1)} %wno_hbm.1, ...), custom_call_target="tpu_custom_call" | custom-call | flops 3657433088 | bytes 8388608 | tf_op jit(solution)/shard_map/mesh_layer/pallas_call | solution.py:360
  30.8 48.8 %hand_over.1 = (f32[256,512]{1,0:T(8,128)}, bf16[1024,512]{1,0:T(8,128)(2,1)}) custom-call(f32[256,512]{1,0:T(8,128)} %get-tuple-element.4.node_in, bf16[1024,512]{1,0:T(8,128)(2,1)} %get-tuple-element.5.edge_in), custom_call_target="tpu_custom_call" | custom-call | tf_op jit(solution)/shard_map/hand_over/pallas_call | solution.py:418

commit v4 on v3

--- a/solution.py
+++ b/solution.py
@@ -159,6 +159,9 @@
     node_bf[...] = node_v[...].astype(BF16)
     near_src[...] = mm(lend_sel[:2 * near, :], node_bf[...]).astype(BF16)
 
+    far_src[...] = packed(
+        mm(lend_sel[2 * near:lent, :], node_bf[...]).astype(BF16)
+    )
     pl.semaphore_wait(barrier, peers)
 
     def near_copy(i, src, dst, ssem, rsem, patch):
@@ -199,12 +202,9 @@
 
     ahead = near_copy(0, near_src, near_in, near_ssem, near_rsem, nxt)
     behind = near_copy(1, near_src, near_in, near_ssem, near_rsem, prv)
+    each_peer(lambda o: far_copy(o, far_src, far_in, far_ssem, far_rsem).start())
     ahead.start()
     behind.start()
-    far_src[...] = packed(
-        mm(lend_sel[2 * near:lent, :], node_bf[...]).astype(BF16)
-    )
-    each_peer(lambda o: far_copy(o, far_src, far_in, far_ssem, far_rsem).start())
     keep_own(far_src, far_in)
 
     indices[2].wait()
@@ -317,19 +317,21 @@
         store.wait()
 
 
-def hand_over(node_in, edge_in, node_out, edge_out, sems):
-    copies = []
-    for a, (src, dst) in enumerate(((edge_in, edge_out), (node_in, node_out))):
+def hand_over(node_in, edge_in, node_out, edge_out, node_v, edge_v, in_sems, out_sems):
+    fetches, stores = [], []
+    for a, (src, mid, dst) in enumerate(((edge_in, edge_v, edge_out), (node_in, node_v, node_out))):
         step = src.shape[0] // PIECES
         for i in range(PIECES):
-            rows = pl.ds(i * step, step)
-            copies.append(pltpu.make_async_copy(
-                src.at[rows], dst.at[rows], sems.at[a * PIECES + i]
-            ))
-    for copy in copies:
-        copy.start()
-    for copy in copies:
-        copy.wait()
+            rows, at = pl.ds(i * step, step), a * PIECES + i
+            fetches.append(pltpu.make_async_copy(src.at[rows], mid.at[rows], in_sems.at[at]))
+            stores.append(pltpu.make_async_copy(mid.at[rows], dst.at[rows], out_sems.at[at]))
+    for fetch in fetches:
+        fetch.start()
+    for fetch, store in zip(fetches, stores):
+        fetch.wait()
+        store.start()
+    for store in stores:
+        store.wait()
 
 
 def per_device(
@@ -420,7 +422,7 @@
         out_shape=tuple(jax.ShapeDtypeStruct(r.shape, r.dtype) for r in results),
         in_specs=[hbm] * 2,
         out_specs=(hbm, hbm),
-        scratch_shapes=[dma((2 * PIECES,))],
+        scratch_shapes=[pltpu.VMEM(r.shape, r.dtype) for r in results] + [dma((2 * PIECES,))] * 2,
         compiler_params=pltpu.CompilerParams(vmem_limit_bytes=62 * 1024 * 1024),
         name="hand_over",
     )(*results))

time: 79.8 us -> 32.2 us (0.40)
  Pallas kernels: 79 us -> 31.4 us
    pallas_call x1, Pallas kernels: 48.8 us -> 2.22 us  [per_device(): pl.pallas_call(hand_over, out_shape=tuple((jax.ShapeDtypeStruct(r.shape,...]
    pallas_call x1, Pallas kernels: 30.2 us -> 29.2 us  [per_device(): pl.pallas_call(functools.partial(layer_kernel, (n_patch, n_sub, n_lane, n...]
where the time goes in v4:
time: 32.2 us; the launch traced here: 32.1 us
  Pallas kernels  31.4 us (98%)
  between operations  0.65 us (2%)
    pallas_call x1, Pallas kernels, per_device(): pl.pallas_call(functools.partial(layer_kernel, (n_patch, n_sub, n_lane, n...  29.2 us
    pallas_call x1, Pallas kernels, per_device(): pl.pallas_call(hand_over, out_shape=tuple((jax.ShapeDtypeStruct(r.shape,...  2.22 us

profile of v4, /device:TPU:1, one launch (start us, length us, event | category | flops | bytes accessed | tf_op | source)
XLA Modules:
  0.0 32.1 jit_solution(11729062506840180550)
XLA Ops:
  0.6 29.2 %mesh_layer.1 = (f32[256,512]{1,0:T(8,128)}, bf16[1024,512]{1,0:T(8,128)(2,1)}) custom-call(f32[256,512]{1,0:T(8,128)} %node_hbm.1, bf16[1024,512]{1,0:T(8,128)(2,1)} %edge_hbm.1, bf16[1536,512]{1,0:T(8,128)(2,1)} %wei_hbm.1, bf16[512,512]{1,0:T(8,128)(2,1)} %weo_hbm.1, bf16[1024,512]{1,0:T(8,128)(2,1)} %wni_hbm.1, bf16[512,512]{1,0:T(8,128)(2,1)} %wno_hbm.1, ...), custom_call_target="tpu_custom_call" | custom-call | flops 3657433088 | bytes 8388608 | tf_op jit(solution)/shard_map/mesh_layer/pallas_call | solution.py:362
  29.8 2.2 %hand_over.1 = (f32[256,512]{1,0:T(8,128)}, bf16[1024,512]{1,0:T(8,128)(2,1)}) custom-call(f32[256,512]{1,0:T(8,128)} %get-tuple-element.4.node_in, bf16[1024,512]{1,0:T(8,128)(2,1)} %get-tuple-element.5.edge_in), custom_call_target="tpu_custom_call" | custom-call | tf_op jit(solution)/shard_map/hand_over/pallas_call | solution.py:420
